TPU v7x, 256 devices: a whole 4x4x8 slice. The times are simulated.
256 devices in a mesh: seq: 32 (over x, z_hi, core), mp: 8 (over z_lo, y).
Axes of the slice: x: 4, y: 4, z: 8 (z_hi: 4, z_lo: 2; z = z_hi * 2 + z_lo), core: 2. Of those that a mesh axis runs over, the one named last changes fastest.
Arguments:
- activations: bfloat16 [131072, 4096], P('seq', 'mp'), may hold values from -6 to 6
- conv_weight: float32 [3, 4096], P(None, 'mp'), may hold values from -3.5 to 3.5
- chan_right: bfloat16 [64, 64, 64], P('mp'), may hold values from -0.75 to 0.75
- chan_left: bfloat16 [64, 64, 64], P('mp'), may hold values from -0.75 to 0.75
- row_factor: bfloat16 [512, 512], replicated, may hold values from -0.25 to 0.25
- col_factor: bfloat16 [256, 256], replicated, may hold values from -0.375 to 0.375
- twiddle_one: float32 [256, 512], P('seq'), may hold values from -2 to 2
- twiddle_two: float32 [256, 512], P(None, 'seq'), may hold values from -2 to 2
- spectrum: bfloat16 [256, 512, 4096], P(None, 'seq', 'mp'), may hold values from -6 to 6
Outputs:
- result: bfloat16 [131072, 4096], P('seq', 'mp')
All inputs are finite; a program needn't handle non-finite values.
Results may differ from a plain program's by a relative error of at most 0.0085.
Values may be sent and summed in bfloat16 or wider, within the bound.
A program may use at most 128 MiB of HBM per device.

v0:
```python
import jax
import jax.numpy as jnp
from jax import lax
from jax.sharding import PartitionSpec as P


def shifted(block, axis, distance):
    devices = range(lax.axis_size(axis))
    route = [(i - distance, i) for i in devices if i - distance in devices]
    return lax.ppermute(block, axis, route)


def shards(
    activations,
    conv_weight,
    chan_right,
    chan_left,
    row_factor,
    col_factor,
    twiddle_one,
    twiddle_two,
    spectrum,
):
    token_count, local_width = activations.shape
    row_count, block_len = twiddle_one.shape
    block_width = chan_right.shape[1]
    local_groups = chan_right.shape[0]
    x_float = activations.astype(jnp.float32)
    carried = shifted(activations[token_count - 2 :], "seq", 1)
    extended = jnp.concatenate([carried.astype(jnp.float32), x_float], axis=0)
    conv_out = (
        conv_weight[0] * extended[2:]
        + conv_weight[1] * extended[1:-1]
        + conv_weight[2] * extended[:-2]
    )
    gated = (x_float * jax.nn.silu(conv_out)).astype(jnp.bfloat16)
    gated = gated.reshape(token_count, local_groups, block_width)
    first = jnp.einsum(
        "nij,ijk->nik", gated, chan_right, preferred_element_type=jnp.float32
    ).astype(jnp.bfloat16)
    turned = lax.all_to_all(first, "mp", split_axis=2, concat_axis=1, tiled=True)
    second = jnp.einsum(
        "nik,kil->nlk", turned, chan_left, preferred_element_type=jnp.float32
    ).astype(jnp.bfloat16)
    natural = lax.all_to_all(second, "mp", split_axis=1, concat_axis=2, tiled=True)
    grid = natural.reshape(row_count, block_len, local_width)
    rows_out = jnp.einsum("pb,abc->apc", row_factor, grid, preferred_element_type=jnp.float32)
    rows_out = (rows_out * twiddle_one[:, :, None]).astype(jnp.bfloat16)
    columns = lax.all_to_all(rows_out, "seq", split_axis=1, concat_axis=0, tiled=True)
    spectral = jnp.einsum("qa,apc->qpc", col_factor, columns, preferred_element_type=jnp.float32)
    spectral = (spectral * spectrum).astype(jnp.bfloat16)
    back = jnp.einsum("qa,qpc->apc", col_factor, spectral, preferred_element_type=jnp.float32)
    back = (back * twiddle_two[:, :, None]).astype(jnp.bfloat16)
    mixed = jnp.einsum(
        "pb,apc->abc",
        row_factor,
        lax.all_to_all(back, "seq", split_axis=0, concat_axis=1, tiled=True),
        preferred_element_type=jnp.float32,
    )
    result = x_float.reshape(row_count, block_len, local_width) + mixed
    return result.astype(jnp.bfloat16).reshape(token_count, local_width)


def solution(mesh):
    in_specs = (
        P("seq", "mp"),
        P(None, "mp"),
        P("mp", None, None),
        P("mp", None, None),
        P(),
        P(),
        P("seq", None),
        P(None, "seq"),
        P(None, "seq", "mp"),
    )
    out_specs = P("seq", "mp")
    return jax.shard_map(shards, mesh=mesh, in_specs=in_specs, out_specs=out_specs, check_vma=False)
```

profile of v0, /device:TPU:1, one launch (start us, length us, event | category | flops | bytes accessed | tf_op | source)
XLA Modules:
  0.0 400.7 jit_solution(10064743188634848485)
XLA Ops:
  1.0 6.3 %collective-permute-start = (bf16[2,512]{0,1:T(8,128)(2,1)S(1)}, bf16[2,512]{0,1:T(8,128)(2,1)S(1)}, u32[]{:S(2)}, u32[]{:S(2)}) collective-permute-start(bf16[2,512]{0,1:T(8,128)(2,1)S(1)} %copy.33), channel_id=1, source_target_pairs={{0,8},{8,16},{16,24},{24,32},{32,40},{40,48},{48,56},{56,64},{64,7... | collective-permute-start | bytes 6152 | tf_op jit(solution)/shard_map/ppermute | solution.py:10
  8.1 6.3 %copy.31 = bf16[4096,512]{0,1:T(8,128)(2,1)} copy(bf16[4096,512]{1,0:T(8,128)(2,1)} %param.9) | data formatting | bytes 8388608 | tf_op args[0]
  14.4 3.3 convert_element_type.39
  17.7 5.6 %multiply_convert_fusion.1 = bf16[4096,512]{0,1:T(8,128)(2,1)S(1)} fusion(f32[4096,512]{0,1:T(8,128)S(1)} %convert_element_type.39, f32[2,512]{0,1:T(8,128)S(1)} %convert_element_type.40, f32[512]{0:T(512)S(1)} %bitcast.72, f32[512]{0:T(512)S(1)} %bitcast.73, f32[512]{0:T(512)S(1)} %bitcast.71), kind=kLoop, calls=%fused_computation.15 | loop fusion | flops 27262976 | bytes 12593152 | tf_op jit(solution)/shard_map/convert_element_type | solution.py:36
  23.3 1.3 fusion.8
  24.6 2.3 copy.35
  26.9 52.8 %all_to_all.69 = bf16[4096,8,64]{0,1,2:T(8,128)(2,1)S(1)} all-to-all(bf16[4096,8,64]{0,1,2:T(8,128)(2,1)S(1)} %copy.35), channel_id=1, replica_groups=mesh['seq'=32,'mp'=8] {'mp'}, dimensions={2} | all-to-all | bytes 8388608 | tf_op jit(solution)/shard_map/all_to_all | solution.py:41
  81.0 2.3 copy.38
  83.3 52.3 %all_to_all.70 = bf16[4096,64,8]{0,2,1:T(8,128)(2,1)S(1)} all-to-all(bf16[4096,64,8]{0,2,1:T(8,128)(2,1)S(1)} %copy.38), channel_id=1, replica_groups=mesh['seq'=32,'mp'=8] {'mp'}, dimensions={1} | all-to-all | bytes 8388608 | tf_op jit(solution)/shard_map/all_to_all | solution.py:45
  136.1 2.2 copy.54
  138.3 5.0 %fusion.10 = bf16[8,512,512]{1,2,0:T(8,128)(2,1)} fusion(f32[8,512]{1,0:T(8,128)S(1)} %copy-done.5, bf16[8,512,512]{1,0,2:T(8,128)(2,1)S(1)} %bitcast.70, bf16[512,512]{1,0:T(8,128)(2,1)S(1)} %copy-done), kind=kOutput, calls=%fused_computation.20 | convolution fusion | flops 2151677952 | bytes 8929280 | tf_op jit(solution)/shard_map/pb,abc->apc/dot_general | solution.py:47
  143.4 8.1 %copy.41 = bf16[8,512,512]{2,0,1:T(8,128)(2,1)} copy(bf16[8,512,512]{1,2,0:T(8,128)(2,1)} %fusion.10) | data formatting | bytes 8388608 | tf_op jit(solution)/shard_map/convert_element_type | solution.py:48
  151.4 11.0 %all-to-all-start.2 = ((bf16[8,512,512]{2,0,1:T(8,128)(2,1)}), bf16[8,512,512]{2,0,1:T(8,128)(2,1)}, u32[]{:S(2)}, u32[]{:S(2)}) async-start(bf16[8,512,512]{2,0,1:T(8,128)(2,1)} %copy.41), calls=%async_computation.2 | async-start | bytes 8388608 | tf_op jit(solution)/shard_map/all_to_all | solution.py:49
  162.5 7.5 %copy.45 = bf16[256,16,512]{0,2,1:T(8,128)(2,1)} copy(bf16[256,16,512]{2,1,0:T(8,128)(2,1)} %param.17) | data formatting | bytes 8388608 | tf_op args[8]
  170.0 88.5 %all-to-all-done.2 = bf16[8,512,512]{2,0,1:T(8,128)(2,1)} async-done(((bf16[8,512,512]{2,0,1:T(8,128)(2,1)}), bf16[8,512,512]{2,0,1:T(8,128)(2,1)}, u32[]{:S(2)}, u32[]{:S(2)}) %all-to-all-start.2) | async-done | bytes 4194336 | tf_op jit(solution)/shard_map/all_to_all | solution.py:49
  258.5 6.0 %copy.43 = bf16[32,8,16,512]{3,2,1,0:T(8,128)(2,1)} copy(bf16[32,8,16,512]{3,1,2,0:T(8,128)(2,1)} %bitcast.16) | data formatting | bytes 8388608 | tf_op jit(solution)/shard_map/all_to_all | solution.py:49
  264.5 14.5 %fusion.6 = bf16[256,16,512]{0,2,1:T(8,128)(2,1)} fusion(f32[256,16]{0,1:T(8,128)S(1)} %copy-done.6, bf16[256,16,512]{0,2,1:T(8,128)(2,1)} %copy.45, bf16[256,16,512]{2,1,0:T(8,128)(2,1)} %bitcast.69, bf16[256,256]{1,0:T(8,128)(2,1)S(1)} %copy-done.4), kind=kOutput, calls=%fused_computation.11 | convolution fusion | flops 2157969408 | bytes 12730368 | tf_op jit(solution)/shard_map/qa,qpc->apc/dot_general | solution.py:52
  279.0 7.9 %copy.46 = bf16[256,16,512]{2,1,0:T(8,128)(2,1)} copy(bf16[256,16,512]{0,2,1:T(8,128)(2,1)} %fusion.6) | data formatting | bytes 8388608 | tf_op jit(solution)/shard_map/convert_element_type | solution.py:53
  286.9 7.5 %all-to-all-start.3 = ((bf16[256,16,512]{2,1,0:T(8,128)(2,1)}), bf16[256,16,512]{2,1,0:T(8,128)(2,1)}, u32[]{:S(2)}, u32[]{:S(2)}) async-start(bf16[256,16,512]{2,1,0:T(8,128)(2,1)} %copy.46), calls=%async_computation.3 | async-start | bytes 8388608 | tf_op jit(solution)/shard_map/all_to_all | solution.py:57
  294.4 7.1 %copy.32 = f32[4096,512]{1,0:T(8,128)} copy(bf16[4096,512]{0,1:T(8,128)(2,1)} %copy.31) | data formatting | bytes 12582912 | tf_op jit(solution)/shard_map/convert_element_type | solution.py:28
  301.5 89.3 %all-to-all-done.3 = bf16[256,16,512]{2,1,0:T(8,128)(2,1)} async-done(((bf16[256,16,512]{2,1,0:T(8,128)(2,1)}), bf16[256,16,512]{2,1,0:T(8,128)(2,1)}, u32[]{:S(2)}, u32[]{:S(2)}) %all-to-all-start.3) | async-done | bytes 4194336 | tf_op jit(solution)/shard_map/all_to_all | solution.py:57
  390.8 2.8 copy.47
  393.6 1.8 copy-done.1
  395.4 5.4 %fusion.5 = bf16[8,512,512]{2,1,0:T(8,128)(2,1)} fusion(f32[8,512,512]{2,1,0:T(8,128)S(1)} %bitcast.63, bf16[8,512,512]{2,1,0:T(8,128)(2,1)S(1)} %bitcast.68, bf16[512,512]{1,0:T(8,128)(2,1)S(1)} %copy-done), kind=kOutput, calls=%fused_computation.9 | convolution fusion | flops 2151677952 | bytes 17301504 | tf_op jit(solution)/shard_map/pb,apc->abc/dot_general | solution.py:54
  (20 shorter events, 3.6 us)
Async XLA Ops:
  0.0 138.3 %copy-start = (bf16[512,512]{1,0:T(8,128)(2,1)S(1)}, bf16[512,512]{1,0:T(8,128)(2,1)}, u32[]{:S(2)}) copy-start(bf16[512,512]{1,0:T(8,128)(2,1)} %param.13) | copy-start | bytes 1572868
  1.0 16.7 %collective-permute-start = (bf16[2,512]{0,1:T(8,128)(2,1)S(1)}, bf16[2,512]{0,1:T(8,128)(2,1)S(1)}, u32[]{:S(2)}, u32[]{:S(2)}) collective-permute-start(bf16[2,512]{0,1:T(8,128)(2,1)S(1)} %copy.33), channel_id=1, source_target_pairs={{0,8},{8,16},{16,24},{24,32},{32,40},{40,48},{48,56},{56,64},{64,7... | collective-permute-start | bytes 6152 | tf_op jit(solution)/shard_map/ppermute | solution.py:10
  17.7 5.6 %copy-start.2 = (bf16[8,64,64]{2,1,0:T(8,128)(2,1)S(1)}, bf16[8,64,64]{2,1,0:T(8,128)(2,1)}, u32[]{:S(2)}) copy-start(bf16[8,64,64]{2,1,0:T(8,128)(2,1)} %param.11) | copy-start | bytes 196612
  26.9 52.8 %copy-start.3 = (bf16[8,64,64]{2,1,0:T(8,128)(2,1)S(1)}, bf16[8,64,64]{2,1,0:T(8,128)(2,1)}, u32[]{:S(2)}) copy-start(bf16[8,64,64]{2,1,0:T(8,128)(2,1)} %param.12) | copy-start | bytes 196612
  136.1 2.3 copy-start.5
  151.4 107.0 %all-to-all-start.2 = ((bf16[8,512,512]{2,0,1:T(8,128)(2,1)}), bf16[8,512,512]{2,0,1:T(8,128)(2,1)}, u32[]{:S(2)}, u32[]{:S(2)}) async-start(bf16[8,512,512]{2,0,1:T(8,128)(2,1)} %copy.41), calls=%async_computation.2 | async-start | bytes 8388608 | tf_op jit(solution)/shard_map/all_to_all | solution.py:49
  258.5 6.0 %copy-start.4 = (bf16[256,256]{1,0:T(8,128)(2,1)S(1)}, bf16[256,256]{1,0:T(8,128)(2,1)}, u32[]{:S(2)}) copy-start(bf16[256,256]{1,0:T(8,128)(2,1)} %param.14) | copy-start | bytes 393220
  258.5 6.0 %copy-start.6 = (f32[256,16]{0,1:T(8,128)S(1)}, f32[256,16]{0,1:T(8,128)}, u32[]{:S(2)}) copy-start(f32[256,16]{0,1:T(8,128)} %param.16) | copy-start | bytes 49156
  286.9 103.8 %all-to-all-start.3 = ((bf16[256,16,512]{2,1,0:T(8,128)(2,1)}), bf16[256,16,512]{2,1,0:T(8,128)(2,1)}, u32[]{:S(2)}, u32[]{:S(2)}) async-start(bf16[256,16,512]{2,1,0:T(8,128)(2,1)} %copy.46), calls=%async_computation.3 | async-start | bytes 8388608 | tf_op jit(solution)/shard_map/all_to_all | solution.py:57
  390.8 4.6 %copy-start.1 = (f32[4096,512]{1,0:T(8,128)S(1)}, f32[4096,512]{1,0:T(8,128)}, u32[]{:S(2)}) copy-start(f32[4096,512]{1,0:T(8,128)} %copy.32) | copy-start | bytes 25165828
where the time goes:
time: 402 us; the launch traced here: 401 us
  waiting for transfers between devices  178 us (44%)
  blocking collectives  105 us (26%)
  local copies, waits for them, and re-layouts  56.7 us (14%)
  matrix products  27.5 us (7%)
  starting transfers between devices  24.8 us (6%)
  other arithmetic  8.86 us (2%)
    all_to_all x1, waiting for transfers between devices, shards(): lax.all_to_all(back, 'seq', split_axis=0, concat_axis=1, tiled=True)  89.3 us
    all_to_all x1, waiting for transfers between devices, shards(): lax.all_to_all(rows_out, 'seq', split_axis=1, concat_axis=0, tiled=True)  88.5 us
    all_to_all x1, blocking collectives, shards(): lax.all_to_all(first, 'mp', split_axis=2, concat_axis=1, tiled=True)  52.8 us
    all_to_all x1, blocking collectives, shards(): lax.all_to_all(second, 'mp', split_axis=1, concat_axis=2, tiled=True)  52.3 us
    unnamed x17, local copies, waits for them, and re-layouts  17.9 us
    dot_general x1, matrix products, shards(): jnp.einsum('qa,qpc->apc', col_factor, spectral, preferred_element_type=jn...  14.5 us
    all_to_all x1, starting transfers between devices, shards(): lax.all_to_all(rows_out, 'seq', split_axis=1, concat_axis=0, tiled=True)  11 us
    convert_element_type x1, local copies, waits for them, and re-layouts, shards(): rows_out = (rows_out * twiddle_one[:, :, None]).astype(jnp.bfloat16)  8.08 us
  transfers between devices with their start and end apart: 3, of which 2 were waited for; matrix products, arithmetic and copies ran while one was open for 6% of the time, Pallas kernels for 0%

commit v1 on v0

v1 whole, which is shorter than its diff:
```python
import jax
import jax.numpy as jnp
from jax import lax
from jax.experimental import pallas as pl
from jax.experimental.pallas import tpu as pltpu
from jax.sharding import PartitionSpec as P

MESH = pl.DeviceIdType.MESH


def shifted(block, axis, distance):
    devices = range(lax.axis_size(axis))
    route = [(i - distance, i) for i in devices if i - distance in devices]
    return lax.ppermute(block, axis, route)


def dot32(a, b):
    return jnp.dot(a, b, preferred_element_type=jnp.float32)


def iota(shape, dim):
    return lax.broadcasted_iota(jnp.int32, shape, dim)


def right_matrix(chan_right):
    groups, width, _ = chan_right.shape
    size = groups * width
    col = iota((width, size), 1)
    spread = (iota((width, size), 0) == col // 128 * 16 + col % 16).astype(jnp.bfloat16)
    full = dot32(chan_right.reshape(size, width), spread)
    same = iota((size, size), 0) // width == iota((size, size), 1) % 128 // 16
    return jnp.where(same, full, 0.0).astype(jnp.bfloat16)


def left_matrices(chan_left):
    width = chan_left.shape[0]
    size = width * 16
    packed = chan_left.reshape(width // 16, 16, width, width).transpose(0, 2, 1, 3)
    spread = (iota((width, size), 0) == iota((width, size), 1) // 16).astype(jnp.bfloat16)
    full = dot32(packed.reshape(width // 16 * size, width), spread)
    full = full.reshape(width // 16, size, size)
    same = iota((size, size), 0) % 16 == iota((size, size), 1) % 16
    return jnp.where(same, full, 0.0).astype(jnp.bfloat16)


def natural_order():
    row, col = iota((512, 512), 0), iota((512, 512), 1)
    target = row // 16 % 8 * 64 + row // 128 * 16 + row % 16
    return (target == col).astype(jnp.bfloat16)


def exchange_kernel(x_ref, out_ref, local_sem, send_sem, recv_sem):
    seq, mp = lax.axis_index("seq"), lax.axis_index("mp")
    me = seq * 8 + mp

    def partner(step):
        z = (seq // 2 % 4) * 2 + mp // 4
        z = (z + step) % 8
        rest = step // 8
        core = (seq + rest) % 2
        x = (seq // 8 + rest // 2) % 4
        y = (mp + rest // 8) % 4
        return (x * 4 + z // 2) * 2 + core, z % 2 * 4 + y

    barrier = pltpu.get_barrier_semaphore()

    @pl.loop(1, 256)
    def _(step):
        pl.semaphore_signal(barrier, inc=1, device_id=partner(step), device_id_type=MESH)

    own = pltpu.make_async_copy(x_ref.at[me], out_ref.at[me], local_sem)
    own.start()
    pl.semaphore_wait(barrier, 255)

    @pl.loop(1, 256)
    def _(step):
        to_seq, to_mp = partner(step)
        pltpu.make_async_remote_copy(
            src_ref=x_ref.at[to_seq * 8 + to_mp],
            dst_ref=out_ref.at[me],
            send_sem=send_sem,
            recv_sem=recv_sem,
            device_id=(to_seq, to_mp),
            device_id_type=MESH,
        ).start()

    own.wait()
    others = out_ref.at[pl.ds(0, 255)]
    pltpu.make_async_copy(others, others, recv_sem).wait()
    pltpu.make_async_copy(others, others, send_sem).wait()


def exchange(x):
    return pl.pallas_call(
        exchange_kernel,
        name="exchange",
        out_shape=jax.ShapeDtypeStruct(x.shape, x.dtype),
        in_specs=[pl.BlockSpec(memory_space=pltpu.VMEM)],
        out_specs=pl.BlockSpec(memory_space=pltpu.VMEM),
        scratch_shapes=[pltpu.SemaphoreType.DMA] * 3,
        compiler_params=pltpu.CompilerParams(
            collective_id=0, has_side_effects=True, vmem_limit_bytes=16 << 20
        ),
    )(x)


def shards(
    activations,
    conv_weight,
    chan_right,
    chan_left,
    row_factor,
    col_factor,
    twiddle_one,
    twiddle_two,
    spectrum,
):
    token_count, local_width = activations.shape
    row_count, block_len = twiddle_one.shape
    x_float = activations.astype(jnp.float32)
    carried = shifted(activations[token_count - 2 :], "seq", 1)
    extended = jnp.concatenate([carried.astype(jnp.float32), x_float], axis=0)
    conv_out = (
        conv_weight[0] * extended[2:]
        + conv_weight[1] * extended[1:-1]
        + conv_weight[2] * extended[:-2]
    )
    gated = (x_float * jax.nn.silu(conv_out)).astype(jnp.bfloat16)
    chan_left = lax.all_gather(chan_left, "mp", tiled=True)
    lefts = left_matrices(chan_left)
    first = dot32(gated, right_matrix(chan_right)).astype(jnp.bfloat16)
    first = first.reshape(row_count, block_len, local_width)
    rows_out = jnp.einsum("pb,abc->apc", row_factor, first, preferred_element_type=jnp.float32)
    rows_out = (rows_out * twiddle_one[:, :, None]).astype(jnp.bfloat16)
    turned = lax.all_to_all(rows_out, "mp", split_axis=0, concat_axis=0, tiled=True)
    parts = []
    for k in range(4):
        block = turned[:, :, k * 128 : (k + 1) * 128].transpose(1, 0, 2).reshape(block_len, 1024)
        parts.append(dot32(block, lefts[k]).astype(jnp.bfloat16).reshape(block_len, 8, 128))
    mixed = jnp.concatenate(parts, axis=2)
    mixed = jnp.einsum("pmc,cd->pmd", mixed, natural_order(), preferred_element_type=jnp.float32)
    mixed = mixed.astype(jnp.bfloat16).reshape(32, 16, 8, 512).transpose(0, 2, 1, 3)
    columns = exchange(mixed.reshape(256, 16, 512))
    spectral = jnp.einsum("qa,apc->qpc", col_factor, columns, preferred_element_type=jnp.float32)
    spectral = (spectral * spectrum).astype(jnp.bfloat16)
    back = jnp.einsum("qa,qpc->apc", col_factor, spectral, preferred_element_type=jnp.float32)
    back = (back * twiddle_two[:, :, None]).astype(jnp.bfloat16)
    back = lax.all_to_all(
        back.reshape(32, 8, 16, 512), "seq", split_axis=0, concat_axis=0, tiled=True
    )
    mixed = jnp.einsum(
        "pb,apc->abc",
        row_factor,
        back.transpose(1, 0, 2, 3).reshape(row_count, block_len, local_width),
        preferred_element_type=jnp.float32,
    )
    result = x_float.reshape(row_count, block_len, local_width) + mixed
    return result.astype(jnp.bfloat16).reshape(token_count, local_width)


def solution(mesh):
    in_specs = (
        P("seq", "mp"),
        P(None, "mp"),
        P("mp", None, None),
        P("mp", None, None),
        P(),
        P(),
        P("seq", None),
        P(None, "seq"),
        P(None, "seq", "mp"),
    )
    out_specs = P("seq", "mp")
    return jax.shard_map(shards, mesh=mesh, in_specs=in_specs, out_specs=out_specs, check_vma=False)
```

time: 402 us -> 407 us (1.012)
  waiting for transfers between devices: 178 us -> 0.01 us
  Pallas kernels: 0 us -> 117 us
  blocking collectives: 105 us -> 175 us
  matrix products: 27.5 us -> 50.2 us
  local copies, waits for them, and re-layouts: 56.7 us -> 34.8 us
  starting transfers between devices: 24.8 us -> 11.8 us
  other arithmetic: 8.86 us -> 17.2 us
    all_to_all x2 -> x1, waiting for transfers between devices: 178 us -> 0.01 us  [shards(): lax.all_to_all(rows_out, 'mp', split_axis=0, concat_axis=0, tiled=True)]
    pallas_call x0 -> x1, Pallas kernels: none -> 117 us  [exchange(): pl.pallas_call(exchange_kernel, name='exchange', out_shape=jax.ShapeDtype...]
    all_gather x0 -> x1, blocking collectives: none -> 69.7 us  [shards(): chan_left = lax.all_gather(chan_left, 'mp', tiled=True)]
    dot_general x4 -> x9, matrix products: 13 us -> 40.8 us  [the longest x6 26 us: dot32(): return jnp.dot(a, b, preferred_element_type=jnp.float32)]
    convert_element_type x5 -> x0, local copies, waits for them, and re-layouts: 27.7 us -> none  [the longest x1 8.08 us: shards(): rows_out = (rows_out * twiddle_one[:, :, None]).astype(jnp.bfloat16)]
    reshape x0 -> x8, local copies, waits for them, and re-layouts: none -> 16.7 us  [the longest x1 12 us: left_matrices(): full = full.reshape(width // 16, size, size)]
    all_to_all x2 -> x1, starting transfers between devices: 18.5 us -> 5.53 us  [shards(): lax.all_to_all(rows_out, 'mp', split_axis=0, concat_axis=0, tiled=True)]
    all_to_all x3 -> x0, local copies, waits for them, and re-layouts: 9.33 us -> none  [the longest x1 6.03 us: shards(): lax.all_to_all(rows_out, 'seq', split_axis=1, concat_axis=0, tiled=True)]
  transfers between devices with their start and end apart: 3 -> 2, of which waited for: 2 -> 0; matrix products, arithmetic and copies ran while one was open for 6% -> 11% of each run, Pallas kernels for 0% -> 0%
where the time goes in v1:
time: 407 us; the launch traced here: 406 us
  blocking collectives  175 us (43%)
  Pallas kernels  117 us (29%)
  matrix products  50.2 us (12%)
  local copies, waits for them, and re-layouts  34.8 us (9%)
  other arithmetic  17.2 us (4%)
  starting transfers between devices  11.8 us (3%)
    pallas_call x1, Pallas kernels, exchange(): pl.pallas_call(exchange_kernel, name='exchange', out_shape=jax.ShapeDtype...  117 us
    all_to_all x1, blocking collectives, shards(): lax.all_to_all(back.reshape(32, 8, 16, 512), 'seq', split_axis=0, concat_...  105 us
    all_gather x1, blocking collectives, shards(): chan_left = lax.all_gather(chan_left, 'mp', tiled=True)  69.7 us
    dot_general x6, matrix products, dot32(): return jnp.dot(a, b, preferred_element_type=jnp.float32)  26 us
    unnamed x21, local copies, waits for them, and re-layouts  12.3 us
    reshape x1, local copies, waits for them, and re-layouts, left_matrices(): full = full.reshape(width // 16, size, size)  12 us
    convert_element_type x1, other arithmetic, left_matrices(): return jnp.where(same, full, 0.0).astype(jnp.bfloat16)  9.42 us
    dot_general x1, matrix products, shards(): jnp.einsum('qa,qpc->apc', col_factor, spectral, preferred_element_type=jn...  9.42 us
  transfers between devices with their start and end apart: 2, of which 0 were waited for; matrix products, arithmetic and copies ran while one was open for 11% of the time, Pallas kernels for 0%

profile of v1, /device:TPU:1, one launch (start us, length us, event | category | flops | bytes accessed | tf_op | source)
XLA Modules:
  0.0 405.7 jit_solution(12310151853852168150)
XLA Ops:
  0.8 6.3 %collective-permute-start = (bf16[2,512]{1,0:T(2,128)(2,1)S(1)}, bf16[2,512]{1,0:T(2,128)(2,1)S(1)}, u32[]{:S(2)}, u32[]{:S(2)}) collective-permute-start(bf16[2,512]{1,0:T(2,128)(2,1)S(1)} %slice.44), channel_id=1, source_target_pairs={{0,8},{8,16},{16,24},{24,32},{32,40},{40,48},{48,56},{56,64},{64,7... | collective-permute-start | bytes 6152 | tf_op jit(solution)/shard_map/ppermute | solution.py:14
  7.9 6.7 %convert_element_type.54 = f32[4096,512]{1,0:T(8,128)} convert(bf16[4096,512]{1,0:T(8,128)(2,1)} %param.9) | non-fusion elementwise | flops 2097152 | bytes 12582912 | tf_op jit(solution)/shard_map/convert_element_type | solution.py:120
  14.6 15.3 %convolution_convert_fusion = bf16[4096,512]{1,0:T(8,128)(2,1)} fusion(f32[4096,512]{1,0:T(8,128)} %convert_element_type.54, f32[2,512]{1,0:T(2,128)S(1)} %convert_element_type.55, f32[512]{0:T(512)S(1)} %bitcast.150, f32[512]{0:T(512)S(1)} %bitcast.151, f32[512]{0:T(512)S(1)} %bitcast.149, bf16[512,64]{1,0:T(8,128)(2,1)S(1)} %bitcast.152, ...), kind=kOutput, calls=%fused_computation.18 | convolution fusion | flops 2215837696 | bytes 12677120 | tf_op jit(solution)/shard_map/dot_general | solution.py:18
  29.9 6.6 %fusion.8 = bf16[8,512,512]{1,2,0:T(8,128)(2,1)} fusion(f32[8,512]{1,0:T(8,128)S(1)} %copy-done.6, bf16[8,512,512]{2,1,0:T(8,128)(2,1)} %bitcast.153, bf16[512,512]{1,0:T(8,128)(2,1)S(1)} %copy-done), kind=kOutput, calls=%fused_computation.19 | convolution fusion | flops 2151677952 | bytes 8929280 | tf_op jit(solution)/shard_map/pb,abc->apc/dot_general | solution.py:133
  36.5 5.5 %all-to-all-start = ((bf16[8,512,512]{1,2,0:T(8,128)(2,1)}), bf16[8,512,512]{1,2,0:T(8,128)(2,1)}, u32[]{:S(2)}, u32[]{:S(2)}) async-start(bf16[8,512,512]{1,2,0:T(8,128)(2,1)} %fusion.8), calls=%async_computation | async-start | bytes 8388608 | tf_op jit(solution)/shard_map/all_to_all | solution.py:135
  42.0 69.7 %all_gather.3 = bf16[64,64,64]{2,1,0:T(8,128)(2,1)S(1)} all-gather(bf16[8,64,64]{2,1,0:T(8,128)(2,1)S(1)} %copy-done.3), channel_id=1, replica_groups=mesh['seq'=32,'mp'=8] {'mp'}, dimensions={0}, use_global_device_ids=true | all-gather | bytes 589824 | tf_op jit(solution)/shard_map/all_gather | solution.py:129
  112.4 7.7 %copy.42 = bf16[256,16,512]{0,2,1:T(8,128)(2,1)} copy(bf16[256,16,512]{2,1,0:T(8,128)(2,1)} %param.17) | data formatting | bytes 8388608 | tf_op args[8]
  120.1 5.6 %convolution_bitcast_fusion = bf16[4096,1024]{0,1:T(8,128)(2,1)} fusion(bf16[4096,64]{1,0:T(8,128)(2,1)S(1)} %bitcast.138, s32[1024]{0:T(1024)S(1)} %get-tuple-element.24, s32[1024]{0:T(1024)S(1)} %get-tuple-element.25, pred[1024]{0:T(1024)(128)(4,1)S(1)} %fusion.121), kind=kOutput, calls=%fused_computation.1 | convolution fusion | flops 537067520 | bytes 8922112 | tf_op jit(solution)/shard_map/dot_general | solution.py:18
  125.7 12.0 %copy.53 = bf16[4096,1024]{1,0:T(8,128)(2,1)} copy(bf16[4096,1024]{0,1:T(8,128)(2,1)} %convolution_bitcast_fusion) | data formatting | bytes 16777216 | tf_op jit(solution)/shard_map/reshape | solution.py:41
  138.8 9.4 %select_convert_fusion = bf16[4,1024,1024]{2,1,0:T(8,128)(2,1)} fusion(bf16[4,1024,1024]{2,1,0:T(8,128)(2,1)} %bitcast.135, pred[1024,1024]{1,0:T(8,128)(4,1)S(1)} %select_compare_fusion), kind=kLoop, calls=%fused_computation | loop fusion | flops 4194304 | bytes 17825792 | tf_op jit(solution)/shard_map/convert_element_type | solution.py:43
  148.2 2.8 fusion.152
  151.0 1.9 copy-done.2
  152.9 1.3 fusion.44
  154.4 1.3 fusion.41
  155.8 1.3 fusion.42
  157.1 1.3 fusion.43
  158.8 2.9 fusion.26
  162.4 116.9 %exchange.1 = bf16[256,16,512]{2,1,0:T(8,128)(2,1)S(1)} custom-call(bf16[256,16,512]{2,1,0:T(8,128)(2,1)S(1)} %bitcast.131), custom_call_target="tpu_custom_call" | custom-call | tf_op jit(solution)/shard_map/exchange/pallas_call | solution.py:94
  279.3 2.0 copy-done.1
  281.2 9.4 %fusion.11 = bf16[32,8,16,512]{3,1,0,2:T(8,128)(2,1)} fusion(f32[256,16]{0,1:T(8,128)S(1)} %copy-done.7, bf16[256,16,512]{0,2,1:T(8,128)(2,1)} %copy.42, bf16[256,16,512]{2,1,0:T(8,128)(2,1)} %copy-done.1, bf16[256,256]{1,0:T(8,128)(2,1)S(1)} %copy-done.5), kind=kOutput, calls=%fused_computation.21 | convolution fusion | flops 2157969408 | bytes 12730368 | tf_op jit(solution)/shard_map/qa,qpc->apc/dot_general | solution.py:146
  290.7 2.6 copy.45
  293.3 104.8 %all_to_all.10 = bf16[32,8,16,512]{3,1,2,0:T(8,128)(2,1)S(1)} all-to-all(bf16[32,8,16,512]{3,1,2,0:T(8,128)(2,1)S(1)} %copy.45), channel_id=1, replica_groups=mesh['seq'=32,'mp'=8] {'seq'}, dimensions={0} | all-to-all | bytes 8388608 | tf_op jit(solution)/shard_map/all_to_all | solution.py:148
  398.2 1.5 copy.46
  400.4 5.4 %fusion.5 = bf16[8,512,512]{2,1,0:T(8,128)(2,1)} fusion(f32[8,512,512]{2,1,0:T(8,128)S(1)} %bitcast.134, bf16[8,512,512]{2,1,0:T(8,128)(2,1)S(1)} %bitcast.137, bf16[512,512]{1,0:T(8,128)(2,1)S(1)} %copy-done), kind=kOutput, calls=%fused_computation.11 | convolution fusion | flops 2151677952 | bytes 17301504 | tf_op jit(solution)/shard_map/pb,apc->abc/dot_general | solution.py:151
  (43 shorter events, 5.5 us)
Async XLA Ops:
  0.0 29.9 %copy-start = (bf16[512,512]{1,0:T(8,128)(2,1)S(1)}, bf16[512,512]{1,0:T(8,128)(2,1)}, u32[]{:S(2)}) copy-start(bf16[512,512]{1,0:T(8,128)(2,1)} %param.13) | copy-start | bytes 1572868
  0.0 14.6 %copy-start.4 = (bf16[8,64,64]{2,1,0:T(8,128)(2,1)S(1)}, bf16[8,64,64]{2,1,0:T(8,128)(2,1)}, u32[]{:S(2)}) copy-start(bf16[8,64,64]{2,1,0:T(8,128)(2,1)} %param.11) | copy-start | bytes 196612
  0.8 13.8 %collective-permute-start = (bf16[2,512]{1,0:T(2,128)(2,1)S(1)}, bf16[2,512]{1,0:T(2,128)(2,1)S(1)}, u32[]{:S(2)}, u32[]{:S(2)}) collective-permute-start(bf16[2,512]{1,0:T(2,128)(2,1)S(1)} %slice.44), channel_id=1, source_target_pairs={{0,8},{8,16},{16,24},{24,32},{32,40},{40,48},{48,56},{56,64},{64,7... | collective-permute-start | bytes 6152 | tf_op jit(solution)/shard_map/ppermute | solution.py:14
  14.6 15.3 %copy-start.6 = (f32[8,512]{1,0:T(8,128)S(1)}, f32[8,512]{1,0:T(8,128)}, u32[]{:S(2)}) copy-start(f32[8,512]{1,0:T(8,128)} %param.15) | copy-start | bytes 49156
  29.9 12.1 %copy-start.3 = (bf16[8,64,64]{2,1,0:T(8,128)(2,1)S(1)}, bf16[8,64,64]{2,1,0:T(8,128)(2,1)}, u32[]{:S(2)}) copy-start(bf16[8,64,64]{2,1,0:T(8,128)(2,1)} %param.12) | copy-start | bytes 196612
  36.5 111.7 %all-to-all-start = ((bf16[8,512,512]{1,2,0:T(8,128)(2,1)}), bf16[8,512,512]{1,2,0:T(8,128)(2,1)}, u32[]{:S(2)}, u32[]{:S(2)}) async-start(bf16[8,512,512]{1,2,0:T(8,128)(2,1)} %fusion.8), calls=%async_computation | async-start | bytes 8388608 | tf_op jit(solution)/shard_map/all_to_all | solution.py:135
  148.2 4.6 %copy-start.2 = (bf16[4,1024,1024]{2,1,0:T(8,128)(2,1)S(1)}, bf16[4,1024,1024]{2,1,0:T(8,128)(2,1)}, u32[]{:S(2)}) copy-start(bf16[4,1024,1024]{2,1,0:T(8,128)(2,1)} %select_convert_fusion) | copy-start | bytes 25165828
  161.7 119.6 %copy-start.5 = (bf16[256,256]{1,0:T(8,128)(2,1)S(1)}, bf16[256,256]{1,0:T(8,128)(2,1)}, u32[]{:S(2)}) copy-start(bf16[256,256]{1,0:T(8,128)(2,1)} %param.14) | copy-start | bytes 393220
  161.7 119.5 %copy-start.7 = (f32[256,16]{0,1:T(8,128)S(1)}, f32[256,16]{0,1:T(8,128)}, u32[]{:S(2)}) copy-start(f32[256,16]{0,1:T(8,128)} %param.16) | copy-start | bytes 49156
  279.3 2.0 copy-start.1
  293.3 106.3 %slice-start = ((s8[8388608]{0:T(1024)(128)(4,1)}), s8[4194304]{0:T(1024)(128)(4,1)S(1)}, s32[]{:S(2)}) async-start(s8[8388608]{0:T(1024)(128)(4,1)} %bitcast.132), calls=%async_computation.2 | async-start | bytes 8388608
  398.2 2.2 slice-start.1

commit v2 on v0

v2 whole, which is shorter than its diff:
```python
import jax
import jax.numpy as jnp
from jax import lax
from jax.experimental import pallas as pl
from jax.experimental.pallas import tpu as pltpu
from jax.sharding import PartitionSpec as P

MESH = pl.DeviceIdType.MESH
BF16 = jnp.bfloat16
F32 = jnp.float32


def dot32(a, b):
    return jnp.dot(a, b, preferred_element_type=F32)


def iota(shape, dim):
    return lax.broadcasted_iota(jnp.int32, shape, dim)


def one_hot(condition):
    return jnp.where(condition, 1.0, 0.0).astype(BF16)


def wait_bytes(ref, sem):
    pltpu.make_async_copy(ref, ref, sem).wait()


def kernel(
    x_hbm,
    taps,
    right_hbm,
    left_hbm,
    row_hbm,
    col_hbm,
    twiddle_one,
    twiddle_two,
    spectrum_hbm,
    out_hbm,
    xw,
    right,
    left_own,
    left_all,
    row_f,
    row_t,
    col_f,
    col_t,
    swap,
    natural,
    right_w,
    left_w,
    twiddle_b,
    gated,
    send_a,
    recv_a,
    mixed,
    send_b,
    recv_b,
    columns,
    kernel_t,
    send_c,
    recv_c,
    load_sem,
    x_sem,
    tail_sem,
    halo_send,
    halo_recv,
    left_send,
    left_recv,
    a_send,
    a_recv,
    a_own,
    b_send,
    b_recv,
    b_own,
    c_send,
    c_recv,
    c_own,
    out_sem,
):
    seq, mp = lax.axis_index("seq"), lax.axis_index("mp")
    x, z_hi, core = seq // 8, seq // 2 % 4, seq % 2
    z_lo, y = mp // 4, mp % 4
    me = seq * 8 + mp

    def partner(step):
        z = (z_hi * 2 + z_lo + step) % 8
        rest = step // 8
        to_core = (core + rest) % 2
        to_x = (x + rest // 2) % 4
        to_y = (y + rest // 8) % 4
        return (to_x * 4 + z // 2) * 2 + to_core, z % 2 * 4 + to_y

    def mp_peer(turn):
        return (z_lo + 1 + turn // 4) % 2 * 4 + (y + turn + 1) % 4

    barrier = pltpu.get_barrier_semaphore()

    small = [
        pltpu.make_async_copy(src, dst, load_sem.at[i])
        for i, (src, dst) in enumerate(
            ((right_hbm, right), (row_hbm, row_f), (col_hbm, col_f), (left_hbm, left_own))
        )
    ]
    for copy in small:
        copy.start()

    def x_copy(a):
        return pltpu.make_async_copy(
            x_hbm.at[pl.ds(pl.multiple_of(a * 512, 512), 512)],
            xw.at[a, pl.ds(16, 512)],
            x_sem.at[a],
        )

    def tail_copy(a):
        return pltpu.make_async_copy(
            x_hbm.at[pl.ds(pl.multiple_of(a * 512 - 16, 16), 16)],
            xw.at[a, pl.ds(0, 16)],
            tail_sem.at[a],
        )

    @pl.loop(0, 8)
    def _(turn):
        a = mp_peer(turn)
        x_copy(a).start()

        @pl.when(a > 0)
        def _():
            tail_copy(a).start()

    kernel_copies = [
        pltpu.make_async_copy(
            spectrum_hbm.at[:, :, pl.ds(256 * ch, 256)], send_c.at[ch], load_sem.at[4 + ch]
        )
        for ch in range(2)
    ]
    for copy in kernel_copies:
        copy.start()

    @pl.loop(1, 256)
    def _(step):
        pl.semaphore_signal(barrier, inc=1, device_id=partner(step), device_id_type=MESH)

    small[0].wait()
    col = iota((64, 512), 1)
    full = dot32(right[...], one_hot(iota((64, 512), 0) == col // 128 * 16 + col % 128 // 8))
    same = iota((512, 512), 0) // 64 == iota((512, 512), 1) % 8
    right_w[...] = jnp.where(same, full, 0.0).astype(BF16)
    small[1].wait()
    small[2].wait()
    small[3].wait()

    pl.semaphore_wait(barrier, 255)
    halo = pltpu.make_async_remote_copy(
        src_ref=x_hbm.at[pl.ds(4080, 16)],
        dst_ref=xw.at[0, pl.ds(0, 16)],
        send_sem=halo_send,
        recv_sem=halo_recv,
        device_id=((seq + 1) % 32, mp),
        device_id_type=MESH,
    )
    halo.start()

    @pl.loop(0, 7)
    def _(turn):
        peer = mp_peer(turn)
        shift = jnp.where(turn < 4, jnp.where(z_lo == 1, 1, 3), 0)
        to_seq = (x * 4 + (z_hi + shift) % 4) * 2 + core
        pltpu.make_async_remote_copy(
            src_ref=left_own,
            dst_ref=left_all.at[mp],
            send_sem=left_send,
            recv_sem=left_recv,
            device_id=(to_seq, peer),
            device_id_type=MESH,
        ).start()

    def rows_at(part):
        return pl.multiple_of((x + part) % 4 * 128, 128)

    def send_rows(turn, part):
        a = mp_peer(turn)
        rows = pl.ds(rows_at(part), 128)
        pltpu.make_async_remote_copy(
            src_ref=send_a.at[a, rows],
            dst_ref=recv_a.at[mp, rows],
            send_sem=a_send,
            recv_sem=a_recv.at[part // 2],
            device_id=(seq, a),
            device_id_type=MESH,
        ).start()

    @pl.loop(0, 8)
    def _(turn):
        a = mp_peer(turn)
        x_copy(a).wait()

        @pl.when(a > 0)
        def _():
            tail_copy(a).wait()

        @pl.when(a == 0)
        def _():
            halo.wait_recv()

            @pl.when(seq == 0)
            def _():
                xw[0, pl.ds(0, 16)] = jnp.zeros((16, 512), BF16)

        @pl.loop(0, 4)
        def _(tile):
            start = pl.multiple_of(tile * 128, 128)
            window = xw[a, pl.ds(start, 144)].astype(F32)
            here = window[16:]
            conv_out = (
                taps[0:1] * here + taps[1:2] * window[15:143] + taps[2:3] * window[14:142]
            )
            gated[pl.ds(start, 128)] = (here * conv_out / (1.0 + jnp.exp(-conv_out))).astype(BF16)

        first = dot32(gated[...], right_w[...]).astype(BF16)
        scale = jnp.sum(jnp.where(iota((512, 8), 1) == a, twiddle_one[...], 0.0), 1, keepdims=True)
        send_a[a] = (dot32(row_f[...], first) * scale).astype(BF16)

        @pl.when(turn < 7)
        def _():
            send_rows(turn, 0)
            send_rows(turn, 1)

    own_rows = pltpu.make_async_copy(send_a.at[mp], recv_a.at[mp], a_own)
    own_rows.start()

    @pl.loop(0, 7)
    def _(turn):
        send_rows(turn, 2)
        send_rows(turn, 3)

    row_t[...] = row_f[...].astype(F32).T.astype(BF16)
    col_t[...] = col_f[...].astype(F32).T.astype(BF16)
    row, col = iota((256, 256), 0), iota((256, 256), 1)
    swap[...] = one_hot(row // 16 + row % 16 * 16 == col)
    row, col = iota((512, 512), 0), iota((512, 512), 1)
    natural[...] = one_hot(row // 16 % 8 * 64 + row // 128 * 16 + row % 16 == col)

    left_all[mp] = left_own[...]
    wait_bytes(left_all.at[pl.ds(0, 7)], left_recv)

    @pl.loop(0, 8)
    def _(owner):
        slab = left_all[owner].astype(F32).reshape(4, 8, 8, 128)
        slab = slab.swapaxes(0, 1).reshape(256, 128).astype(BF16)
        for u in range(2):
            spread = iota((128, 1024), 0) == iota((128, 1024), 1) // 16 + 64 * u
            full = dot32(slab, one_hot(spread))
            k = owner % 2 * 8 + 4 * u + iota((256, 1024), 0) // 8 % 4
            full = jnp.where(k == iota((256, 1024), 1) % 16, full, 0.0).astype(BF16)
            rows = pl.ds(pl.multiple_of((owner % 2 * 2 + u) * 32, 32), 32)
            left_w[owner // 2, :, rows] = full.reshape(8, 32, 1024)

    for ch in range(2):
        kernel_copies[ch].wait()

        @pl.loop(0, 16)
        def _(block):
            rows = pl.ds(pl.multiple_of(block * 16, 16), 16)
            turned = dot32(swap[...], send_c[ch, rows].reshape(256, 256)).astype(BF16)
            kernel_t[ch, :, rows] = turned.reshape(16, 16, 256)

    for p in range(16):
        twiddle_b[p] = jnp.broadcast_to(twiddle_two[:, p : p + 1], (256, 128))

    own_rows.wait()

    def send_columns(ch, half, to_mp):
        @pl.loop(0, 16)
        def _(i):
            part = 2 * half + i // 8
            to_z = (z_hi + i // 2) % 4
            to_core = (core + i) % 2
            to_seq = ((x + part) % 4 * 4 + to_z) * 2 + to_core
            rows = pl.ds(pl.multiple_of((to_z * 2 + to_core) * 16, 16), 16)
            src = send_b.at[ch, to_mp, part, rows]
            dst = recv_b.at[ch, me]
            own = jnp.logical_and(to_seq == seq, to_mp == mp)

            @pl.when(own)
            def _():
                pltpu.make_async_copy(src, dst, b_own.at[ch]).start()

            @pl.when(jnp.logical_not(own))
            def _():
                pltpu.make_async_remote_copy(
                    src_ref=src,
                    dst_ref=dst,
                    send_sem=b_send,
                    recv_sem=b_recv.at[ch],
                    device_id=(to_seq, to_mp),
                    device_id_type=MESH,
                ).start()

    for half in range(2):
        wait_bytes(recv_a.at[pl.ds(0, 7), pl.ds(0, 256)], a_recv.at[half])

        @pl.loop(0, 4)
        def _(group):
            lanes = pl.ds(pl.multiple_of(group * 128, 128), 128)
            block = jnp.concatenate(
                [
                    jnp.concatenate(
                        [recv_a[m, pl.ds(rows_at(2 * half + i), 128), lanes] for i in range(2)], 0
                    )
                    for m in range(8)
                ],
                1,
            )
            for n in range(4):
                cut = slice(256 * n, 256 * n + 256)
                weights = left_w[group, :, :, cut].reshape(1024, 256)
                mixed[group, :, cut] = dot32(block, weights).astype(BF16)

        @pl.loop(0, 8)
        def _(turn):
            to_mp = mp_peer(turn)
            lanes = pl.ds(pl.multiple_of(to_mp * 128, 128), 128)
            block = jnp.concatenate([mixed[group, :, lanes] for group in range(4)], 1)
            for ch in range(2):
                cut = slice(256 * ch, 256 * ch + 256)
                turned = dot32(block, natural[:, cut]).astype(BF16)
                send_b[ch, to_mp, pl.ds(2 * half, 2)] = turned.reshape(2, 128, 256)
            send_columns(0, half, to_mp)

        @pl.loop(0, 8)
        def _(turn):
            send_columns(1, half, mp_peer(turn))

    for ch in range(2):
        wait_bytes(recv_b.at[ch, pl.ds(0, 255)], b_recv.at[ch])
        wait_bytes(recv_b.at[ch, 0], b_own.at[ch])

        @pl.loop(0, 16)
        def _(block):
            rows = pl.ds(pl.multiple_of(block * 16, 16), 16)
            turned = dot32(swap[...], recv_b[ch, rows].reshape(256, 256)).astype(BF16)
            columns[:, rows] = turned.reshape(16, 16, 256)

        @pl.loop(0, 16)
        def _(p):
            spectral = (dot32(col_f[...], columns[p]) * kernel_t[ch, p].astype(F32)).astype(BF16)
            back = dot32(col_t[...], spectral)
            scale = twiddle_b[p]
            columns[p] = (back * jnp.concatenate([scale, scale], 1)).astype(BF16)

        @pl.loop(0, 16)
        def _(i):
            block = (seq // 2 + i) % 16
            rows = pl.ds(pl.multiple_of(block * 16, 16), 16)
            turned = dot32(swap[...], columns[:, rows].reshape(256, 256)).astype(BF16)
            send_c[ch, rows] = turned.reshape(16, 16, 256)
            for to_core in range(2):
                to_seq = block * 2 + to_core
                src = send_c.at[ch, pl.ds(pl.multiple_of(to_seq * 8, 8), 8)]
                dst = recv_c.at[ch, :, pl.ds(pl.multiple_of(seq * 16, 16), 16)]

                @pl.when(to_seq == seq)
                def _(src=src, dst=dst):
                    pltpu.make_async_copy(src, dst, c_own.at[ch]).start()

                @pl.when(to_seq != seq)
                def _(src=src, dst=dst, to_seq=to_seq):
                    pltpu.make_async_remote_copy(
                        src_ref=src,
                        dst_ref=dst,
                        send_sem=c_send,
                        recv_sem=c_recv.at[ch],
                        device_id=(to_seq, mp),
                        device_id_type=MESH,
                    ).start()

    wait_bytes(send_a.at[pl.ds(0, 7)], a_send)

    def out_copy(ch, a):
        lanes = pl.ds(256 * ch, 256)
        return pltpu.make_async_copy(
            send_a.at[a, :, lanes],
            out_hbm.at[pl.ds(pl.multiple_of(a * 512, 512), 512), lanes],
            out_sem.at[ch, a],
        )

    for ch in range(2):
        wait_bytes(recv_c.at[ch, :, pl.ds(0, 496)], c_recv.at[ch])
        wait_bytes(recv_c.at[ch, :, pl.ds(0, 16)], c_own.at[ch])

        @pl.loop(0, 8)
        def _(a):
            cut = slice(256 * ch, 256 * ch + 256)
            total = dot32(row_t[...], recv_c[ch, a])
            send_a[a, :, cut] = (xw[a, 16:, cut].astype(F32) + total).astype(BF16)
            out_copy(ch, a).start()

    for ch in range(2):

        @pl.loop(0, 8)
        def _(a):
            out_copy(ch, a).wait()

    halo.wait_send()
    wait_bytes(left_all.at[pl.ds(0, 7)], left_send)
    wait_bytes(recv_b.at[0, pl.ds(0, 255)], b_send)
    wait_bytes(recv_b.at[1, pl.ds(0, 255)], b_send)
    wait_bytes(recv_c.at[0, :, pl.ds(0, 496)], c_send)
    wait_bytes(recv_c.at[1, :, pl.ds(0, 496)], c_send)


def shards(
    activations,
    conv_weight,
    chan_right,
    chan_left,
    row_factor,
    col_factor,
    twiddle_one,
    twiddle_two,
    spectrum,
):
    any_space = pl.BlockSpec(memory_space=pl.ANY)
    vmem = pl.BlockSpec(memory_space=pltpu.VMEM)
    packed = chan_left.reshape(2, 4, 64, 64).transpose(1, 2, 0, 3).reshape(4, 64, 128)
    dma = pltpu.SemaphoreType.DMA
    scratch = [
        ((8, 528, 512), BF16),
        ((512, 64), BF16),
        ((4, 64, 128), BF16),
        ((8, 4, 64, 128), BF16),
        ((512, 512), BF16),
        ((512, 512), BF16),
        ((256, 256), BF16),
        ((256, 256), BF16),
        ((256, 256), BF16),
        ((512, 512), BF16),
        ((512, 512), BF16),
        ((4, 8, 128, 1024), BF16),
        ((16, 256, 128), F32),
        ((512, 512), BF16),
        ((8, 512, 512), BF16),
        ((8, 512, 512), BF16),
        ((4, 256, 1024), BF16),
        ((2, 8, 4, 128, 256), BF16),
        ((2, 256, 16, 256), BF16),
        ((16, 256, 256), BF16),
        ((2, 16, 256, 256), BF16),
        ((2, 256, 16, 256), BF16),
        ((2, 8, 512, 256), BF16),
    ]
    sems = [(6,), (8,), (8,), (), (), (), (), (), (2,), (), (), (2,), (2,), (), (2,), (2,), (2, 8)]
    return pl.pallas_call(
        kernel,
        name="monarch",
        out_shape=jax.ShapeDtypeStruct(activations.shape, activations.dtype),
        in_specs=[any_space, vmem, any_space, any_space, any_space, any_space, vmem, vmem, any_space],
        out_specs=any_space,
        scratch_shapes=[pltpu.VMEM(*one) for one in scratch]
        + [dma(shape) if shape else dma for shape in sems],
        compiler_params=pltpu.CompilerParams(
            collective_id=0, has_side_effects=True, vmem_limit_bytes=60 << 20
        ),
    )(
        activations,
        conv_weight,
        chan_right.reshape(512, 64),
        packed,
        row_factor,
        col_factor,
        twiddle_one.T,
        twiddle_two,
        spectrum,
    )


def solution(mesh):
    in_specs = (
        P("seq", "mp"),
        P(None, "mp"),
        P("mp", None, None),
        P("mp", None, None),
        P(),
        P(),
        P("seq", None),
        P(None, "seq"),
        P(None, "seq", "mp"),
    )
    out_specs = P("seq", "mp")
    return jax.shard_map(shards, mesh=mesh, in_specs=in_specs, out_specs=out_specs, check_vma=False)
```

time: 402 us -> 273 us (0.68)
  Pallas kernels: 0 us -> 262 us
  waiting for transfers between devices: 178 us -> 0 us
  blocking collectives: 105 us -> 0 us
  local copies, waits for them, and re-layouts: 56.7 us -> 9.26 us
  matrix products: 27.5 us -> 0 us
  starting transfers between devices: 24.8 us -> 0 us
  other arithmetic: 8.86 us -> 0 us
    pallas_call x0 -> x1, Pallas kernels: none -> 262 us  [shards(): pl.pallas_call(kernel, name='monarch', out_shape=jax.ShapeDtypeStruct(act...]
    all_to_all x2 -> x0, waiting for transfers between devices: 178 us -> none  [the longest x1 89.3 us: shards(): lax.all_to_all(back, 'seq', split_axis=0, concat_axis=1, tiled=True)]
    all_to_all x2 -> x0, blocking collectives: 105 us -> none  [the longest x1 52.8 us: shards(): lax.all_to_all(first, 'mp', split_axis=2, concat_axis=1, tiled=True)]
    convert_element_type x5 -> x0, local copies, waits for them, and re-layouts: 27.7 us -> none  [the longest x1 8.08 us: shards(): rows_out = (rows_out * twiddle_one[:, :, None]).astype(jnp.bfloat16)]
    dot_general x5 -> x0, matrix products: 27.5 us -> none  [the longest x1 14.5 us: shards(): jnp.einsum('qa,qpc->apc', col_factor, spectral, preferred_element_type=jn...]
    all_to_all x2 -> x0, starting transfers between devices: 18.5 us -> none  [the longest x1 11 us: shards(): lax.all_to_all(rows_out, 'seq', split_axis=1, concat_axis=0, tiled=True)]
    unnamed x17 -> x3, local copies, waits for them, and re-layouts: 17.9 us -> 7.48 us
    all_to_all x3 -> x0, local copies, waits for them, and re-layouts: 9.33 us -> none  [the longest x1 6.03 us: shards(): lax.all_to_all(rows_out, 'seq', split_axis=1, concat_axis=0, tiled=True)]
  transfers between devices with their start and end apart: 3 -> 0, of which waited for: 2 -> 0; matrix products, arithmetic and copies ran while one was open for 6% -> 0% of each run, Pallas kernels for 0% -> 0%
where the time goes in v2:
time: 273 us; the launch traced here: 272 us
  Pallas kernels  262 us (96%)
  local copies, waits for them, and re-layouts  9.26 us (3%)
    pallas_call x1, Pallas kernels, shards(): pl.pallas_call(kernel, name='monarch', out_shape=jax.ShapeDtypeStruct(act...  262 us
    unnamed x3, local copies, waits for them, and re-layouts  7.48 us

profile of v2, /device:TPU:1, one launch (start us, length us, event | category | flops | bytes accessed | tf_op | source)
XLA Modules:
  0.0 271.5 jit_solution(6697425419417254348)
XLA Ops:
  0.0 1.0 copy.14
  1.0 0.7 reshape.11.left_hbm
  1.8 1.5 copy.12.twiddle_two
  3.2 1.6 copy.11
  4.8 262.3 %monarch.1 = bf16[4096,512]{1,0:T(8,128)(2,1)} custom-call(bf16[4096,512]{1,0:T(8,128)(2,1)} %x_hbm.1, f32[3,512]{1,0:T(4,128)} %taps.1, bf16[512,64]{1,0:T(8,128)(2,1)} %bitcast.8, bf16[4,64,128]{2,1,0:T(8,128)(2,1)} %reshape.11.left_hbm, bf16[512,512]{1,0:T(8,128)(2,1)} %row_hbm.1, bf16[256,256]{1,0:T(8,128)(2,1)} %col_hbm.1, f32[512,8]{1,0:T(8,128)} %bitcast.6, ...), custom_call_target="tpu_custom_call" | custom-call | tf_op jit(solution)/shard_map/monarch/pallas_call | solution.py:454
  267.1 4.5 %copy.16 = bf16[4096,512]{1,0:T(8,128)(2,1)} copy(bf16[4096,512]{1,0:T(8,128)(2,1)} %monarch.1) | data formatting | bytes 8388608

commit v3 on v2

--- a/solution.py
+++ b/solution.py
@@ -39,8 +39,10 @@
     out_hbm,
     xw,
     right,
+    left_raw,
     left_own,
     left_all,
+    row_n,
     row_f,
     row_t,
     col_f,
@@ -49,6 +51,8 @@
     natural,
     right_w,
     left_w,
+    twiddle_n,
+    twiddle_a,
     twiddle_b,
     gated,
     send_a,
@@ -60,7 +64,9 @@
     kernel_t,
     send_c,
     recv_c,
+    ready,
     load_sem,
+    row_sem,
     x_sem,
     tail_sem,
     halo_send,
@@ -83,26 +89,38 @@
     z_lo, y = mp // 4, mp % 4
     me = seq * 8 + mp
 
-    def partner(step):
-        z = (z_hi * 2 + z_lo + step) % 8
-        rest = step // 8
-        to_core = (core + rest) % 2
-        to_x = (x + rest // 2) % 4
-        to_y = (y + rest // 8) % 4
-        return (to_x * 4 + z // 2) * 2 + to_core, z % 2 * 4 + to_y
-
     def mp_peer(turn):
         return (z_lo + 1 + turn // 4) % 2 * 4 + (y + turn + 1) % 4
 
     barrier = pltpu.get_barrier_semaphore()
+
+    @pl.loop(0, 7)
+    def _(turn):
+        peer = (seq, mp_peer(turn))
+        pl.semaphore_signal(barrier, inc=1, device_id=peer, device_id_type=MESH)
 
     small = [
         pltpu.make_async_copy(src, dst, load_sem.at[i])
         for i, (src, dst) in enumerate(
-            ((right_hbm, right), (row_hbm, row_f), (col_hbm, col_f), (left_hbm, left_own))
+            ((right_hbm, right), (row_hbm, row_n), (col_hbm, col_f), (left_hbm, left_raw))
         )
     ]
     for copy in small:
+        copy.start()
+
+    blocks = [(2, 0), (2, 1), (1, 0), (1, 1), (1, 2), (1, 3), (0, 0), (0, 1)]
+    blocks += [(2, 2), (2, 3), (3, 0), (3, 1), (3, 2), (3, 3), (0, 2), (0, 3)]
+
+    def block_rows(i):
+        up, along = blocks[i]
+        start = (x + along) % 4 * 128 + (z_hi + up) % 4 * 32
+        return pl.ds(pl.multiple_of(start, 32), 32)
+
+    row_copies = [
+        pltpu.make_async_copy(row_hbm.at[block_rows(i)], row_f.at[pl.ds(32 * i, 32)], row_sem.at[i])
+        for i in range(16)
+    ]
+    for copy in row_copies:
         copy.start()
 
     def x_copy(a):
@@ -119,9 +137,12 @@
             tail_sem.at[a],
         )
 
+    def front_row(step):
+        return (y + 1 + step // 2) % 4 * 2 + step % 2
+
     @pl.loop(0, 8)
-    def _(turn):
-        a = mp_peer(turn)
+    def _(step):
+        a = front_row(step)
         x_copy(a).start()
 
         @pl.when(a > 0)
@@ -137,20 +158,31 @@
     for copy in kernel_copies:
         copy.start()
 
-    @pl.loop(1, 256)
+    @pl.loop(1, 32)
     def _(step):
-        pl.semaphore_signal(barrier, inc=1, device_id=partner(step), device_id_type=MESH)
+        peer = ((seq + step) % 32, mp)
+        pl.semaphore_signal(barrier, inc=1, device_id=peer, device_id_type=MESH)
 
     small[0].wait()
     col = iota((64, 512), 1)
     full = dot32(right[...], one_hot(iota((64, 512), 0) == col // 128 * 16 + col % 128 // 8))
     same = iota((512, 512), 0) // 64 == iota((512, 512), 1) % 8
     right_w[...] = jnp.where(same, full, 0.0).astype(BF16)
-    small[1].wait()
-    small[2].wait()
-    small[3].wait()
-
-    pl.semaphore_wait(barrier, 255)
+    for copy in small[1:] + row_copies:
+        copy.wait()
+    for kk in range(4):
+        left_own[kk] = jnp.concatenate([left_raw[kk], left_raw[4 + kk]], 1)
+    twiddle_n[...] = twiddle_one[...].T
+    for i in range(16):
+        twiddle_a[32 * i : 32 * i + 32] = twiddle_n[block_rows(i)]
+
+    pl.semaphore_wait(barrier, 38)
+
+    @pl.loop(0, 7)
+    def _(turn):
+        peer = (seq, mp_peer(turn))
+        pl.semaphore_signal(ready, inc=1, device_id=peer, device_id_type=MESH)
+
     halo = pltpu.make_async_remote_copy(
         src_ref=x_hbm.at[pl.ds(4080, 16)],
         dst_ref=xw.at[0, pl.ds(0, 16)],
@@ -161,38 +193,44 @@
     )
     halo.start()
 
-    @pl.loop(0, 7)
-    def _(turn):
-        peer = mp_peer(turn)
-        shift = jnp.where(turn < 4, jnp.where(z_lo == 1, 1, 3), 0)
-        to_seq = (x * 4 + (z_hi + shift) % 4) * 2 + core
-        pltpu.make_async_remote_copy(
-            src_ref=left_own,
-            dst_ref=left_all.at[mp],
-            send_sem=left_send,
-            recv_sem=left_recv,
-            device_id=(to_seq, peer),
-            device_id_type=MESH,
-        ).start()
-
-    def rows_at(part):
-        return pl.multiple_of((x + part) % 4 * 128, 128)
-
-    def send_rows(turn, part):
-        a = mp_peer(turn)
-        rows = pl.ds(rows_at(part), 128)
-        pltpu.make_async_remote_copy(
-            src_ref=send_a.at[a, rows],
-            dst_ref=recv_a.at[mp, rows],
-            send_sem=a_send,
-            recv_sem=a_recv.at[part // 2],
-            device_id=(seq, a),
-            device_id_type=MESH,
-        ).start()
+    def send_left():
+        @pl.loop(0, 7)
+        def _(turn):
+            peer = mp_peer(turn)
+            shift = jnp.where(turn < 4, jnp.where(z_lo == 1, 1, 3), 0)
+            to_seq = (x * 4 + (z_hi + shift) % 4) * 2 + core
+            pltpu.make_async_remote_copy(
+                src_ref=left_own,
+                dst_ref=left_all.at[mp],
+                send_sem=left_send,
+                recv_sem=left_recv,
+                device_id=(to_seq, peer),
+                device_id_type=MESH,
+            ).start()
+
+    def send_rows(step, part):
+        a = front_row(step)
+
+        def send(to_z):
+            rows = pl.ds(pl.multiple_of((1 - to_z) * 256 + part * 64, 64), 64)
+            pltpu.make_async_remote_copy(
+                src_ref=send_a.at[a, rows],
+                dst_ref=recv_a.at[mp, step % 2, pl.ds(part * 64, 64)],
+                send_sem=a_send,
+                recv_sem=a_recv.at[part],
+                device_id=(seq, to_z * 4 + a // 2),
+                device_id_type=MESH,
+            ).start()
+
+        send(1 - z_lo)
+
+        @pl.when(step < 6)
+        def _():
+            send(z_lo)
 
     @pl.loop(0, 8)
-    def _(turn):
-        a = mp_peer(turn)
+    def _(step):
+        a = front_row(step)
         x_copy(a).wait()
 
         @pl.when(a > 0)
@@ -218,23 +256,29 @@
             gated[pl.ds(start, 128)] = (here * conv_out / (1.0 + jnp.exp(-conv_out))).astype(BF16)
 
         first = dot32(gated[...], right_w[...]).astype(BF16)
-        scale = jnp.sum(jnp.where(iota((512, 8), 1) == a, twiddle_one[...], 0.0), 1, keepdims=True)
+        scale = jnp.sum(jnp.where(iota((512, 8), 1) == a, twiddle_a[...], 0.0), 1, keepdims=True)
         send_a[a] = (dot32(row_f[...], first) * scale).astype(BF16)
 
-        @pl.when(turn < 7)
-        def _():
-            send_rows(turn, 0)
-            send_rows(turn, 1)
-
-    own_rows = pltpu.make_async_copy(send_a.at[mp], recv_a.at[mp], a_own)
+        send_rows(step, 0)
+
+        @pl.when(step == 1)
+        def _():
+            pl.semaphore_wait(ready, 7)
+            send_left()
+
+    own_rows = pltpu.make_async_copy(
+        send_a.at[pl.ds(pl.multiple_of(2 * y, 2), 2), pl.ds(pl.multiple_of((1 - z_lo) * 256, 256), 256)],
+        recv_a.at[mp],
+        a_own,
+    )
     own_rows.start()
-
-    @pl.loop(0, 7)
-    def _(turn):
-        send_rows(turn, 2)
-        send_rows(turn, 3)
-
-    row_t[...] = row_f[...].astype(F32).T.astype(BF16)
+    for part in range(1, 4):
+
+        @pl.loop(0, 8)
+        def _(step):
+            send_rows(step, part)
+
+    row_t[...] = row_n[...].astype(F32).T.astype(BF16)
     col_t[...] = col_f[...].astype(F32).T.astype(BF16)
     row, col = iota((256, 256), 0), iota((256, 256), 1)
     swap[...] = one_hot(row // 16 + row % 16 * 16 == col)
@@ -265,49 +309,58 @@
             turned = dot32(swap[...], send_c[ch, rows].reshape(256, 256)).astype(BF16)
             kernel_t[ch, :, rows] = turned.reshape(16, 16, 256)
 
+    scales = twiddle_two[...].T
     for p in range(16):
-        twiddle_b[p] = jnp.broadcast_to(twiddle_two[:, p : p + 1], (256, 128))
+        twiddle_b[p] = jnp.broadcast_to(scales[:, p : p + 1], (256, 128))
 
     own_rows.wait()
 
-    def send_columns(ch, half, to_mp):
-        @pl.loop(0, 16)
+    first_a = pl.multiple_of(seq * 8 + y * 2, 2)
+
+    def send_columns(ch, part, to_mp):
+        up = [2, 3 - 2 * z_lo, 3 - 2 * z_lo, 0][part]
+        along = [2 - 2 * z_lo, 0, 2, 2 - 2 * z_lo][part]
+
+        @pl.loop(0, 4)
         def _(i):
-            part = 2 * half + i // 8
-            to_z = (z_hi + i // 2) % 4
             to_core = (core + i) % 2
-            to_seq = ((x + part) % 4 * 4 + to_z) * 2 + to_core
-            rows = pl.ds(pl.multiple_of((to_z * 2 + to_core) * 16, 16), 16)
-            src = send_b.at[ch, to_mp, part, rows]
-            dst = recv_b.at[ch, me]
-            own = jnp.logical_and(to_seq == seq, to_mp == mp)
-
-            @pl.when(own)
-            def _():
-                pltpu.make_async_copy(src, dst, b_own.at[ch]).start()
-
-            @pl.when(jnp.logical_not(own))
-            def _():
+            to_seq = ((x + along + i // 2) % 4 * 4 + (z_hi + up) % 4) * 2 + to_core
+            rows = pl.ds(pl.multiple_of(part * 64 + i // 2 * 32 + to_core * 16, 16), 16)
+            src = send_b.at[ch, to_mp, :, rows]
+            dst = recv_b.at[ch, pl.ds(first_a, 2)]
+
+            def remote():
                 pltpu.make_async_remote_copy(
                     src_ref=src,
                     dst_ref=dst,
-                    send_sem=b_send,
+                    send_sem=b_send.at[ch],
                     recv_sem=b_recv.at[ch],
                     device_id=(to_seq, to_mp),
                     device_id_type=MESH,
                 ).start()
 
-    for half in range(2):
-        wait_bytes(recv_a.at[pl.ds(0, 7), pl.ds(0, 256)], a_recv.at[half])
+            if part < 3:
+                remote()
+            else:
+                own = jnp.logical_and(to_seq == seq, to_mp == mp)
+
+                @pl.when(own)
+                def _():
+                    pltpu.make_async_copy(src, dst, b_own.at[ch]).start()
+
+                @pl.when(jnp.logical_not(own))
+                def _():
+                    remote()
+
+    for part in range(4):
+        wait_bytes(recv_a.at[pl.ds(0, 7), :, pl.ds(0, 64)], a_recv.at[part])
 
         @pl.loop(0, 4)
         def _(group):
             lanes = pl.ds(pl.multiple_of(group * 128, 128), 128)
             block = jnp.concatenate(
                 [
-                    jnp.concatenate(
-                        [recv_a[m, pl.ds(rows_at(2 * half + i), 128), lanes] for i in range(2)], 0
-                    )
+                    recv_a[m, :, 64 * part : 64 * part + 64, lanes].reshape(128, 128)
                     for m in range(8)
                 ],
                 1,
@@ -325,16 +378,25 @@
             for ch in range(2):
                 cut = slice(256 * ch, 256 * ch + 256)
                 turned = dot32(block, natural[:, cut]).astype(BF16)
-                send_b[ch, to_mp, pl.ds(2 * half, 2)] = turned.reshape(2, 128, 256)
-            send_columns(0, half, to_mp)
-
-        @pl.loop(0, 8)
-        def _(turn):
-            send_columns(1, half, mp_peer(turn))
+                send_b[ch, to_mp, :, 64 * part : 64 * part + 64] = turned.reshape(2, 64, 256)
+            send_columns(0, part, to_mp)
+
+        for late in {0: [0], 3: [1, 2, 3]}.get(part, []):
+
+            @pl.loop(0, 8)
+            def _(turn):
+                send_columns(1, late, mp_peer(turn))
 
     for ch in range(2):
-        wait_bytes(recv_b.at[ch, pl.ds(0, 255)], b_recv.at[ch])
-        wait_bytes(recv_b.at[ch, 0], b_own.at[ch])
+        @pl.when(z_lo == 1)
+        def _():
+            wait_bytes(recv_b.at[ch, pl.ds(0, 254)], b_recv.at[ch])
+            wait_bytes(recv_b.at[ch, pl.ds(0, 2)], b_own.at[ch])
+
+        @pl.when(z_lo == 0)
+        def _():
+            wait_bytes(recv_b.at[ch], b_recv.at[ch])
+
 
         @pl.loop(0, 16)
         def _(block):
@@ -375,7 +437,7 @@
                         device_id_type=MESH,
                     ).start()
 
-    wait_bytes(send_a.at[pl.ds(0, 7)], a_send)
+    wait_bytes(recv_a.at[pl.ds(0, 7)], a_send)
 
     def out_copy(ch, a):
         lanes = pl.ds(256 * ch, 256)
@@ -404,8 +466,16 @@
 
     halo.wait_send()
     wait_bytes(left_all.at[pl.ds(0, 7)], left_send)
-    wait_bytes(recv_b.at[0, pl.ds(0, 255)], b_send)
-    wait_bytes(recv_b.at[1, pl.ds(0, 255)], b_send)
+    for ch in range(2):
+
+        @pl.when(z_lo == 1)
+        def _():
+            wait_bytes(recv_b.at[ch, pl.ds(0, 254)], b_send.at[ch])
+
+        @pl.when(z_lo == 0)
+        def _():
+            wait_bytes(recv_b.at[ch], b_send.at[ch])
+
     wait_bytes(recv_c.at[0, :, pl.ds(0, 496)], c_send)
     wait_bytes(recv_c.at[1, :, pl.ds(0, 496)], c_send)
 
@@ -423,13 +493,14 @@
 ):
     any_space = pl.BlockSpec(memory_space=pl.ANY)
     vmem = pl.BlockSpec(memory_space=pltpu.VMEM)
-    packed = chan_left.reshape(2, 4, 64, 64).transpose(1, 2, 0, 3).reshape(4, 64, 128)
     dma = pltpu.SemaphoreType.DMA
     scratch = [
         ((8, 528, 512), BF16),
         ((512, 64), BF16),
+        ((8, 64, 64), BF16),
         ((4, 64, 128), BF16),
         ((8, 4, 64, 128), BF16),
+        ((512, 512), BF16),
         ((512, 512), BF16),
         ((512, 512), BF16),
         ((256, 256), BF16),
@@ -438,19 +509,21 @@
         ((512, 512), BF16),
         ((512, 512), BF16),
         ((4, 8, 128, 1024), BF16),
+        ((512, 8), F32),
+        ((512, 8), F32),
         ((16, 256, 128), F32),
         ((512, 512), BF16),
         ((8, 512, 512), BF16),
-        ((8, 512, 512), BF16),
-        ((4, 256, 1024), BF16),
-        ((2, 8, 4, 128, 256), BF16),
+        ((8, 2, 256, 512), BF16),
+        ((4, 128, 1024), BF16),
+        ((2, 8, 2, 256, 256), BF16),
         ((2, 256, 16, 256), BF16),
         ((16, 256, 256), BF16),
         ((2, 16, 256, 256), BF16),
         ((2, 256, 16, 256), BF16),
         ((2, 8, 512, 256), BF16),
     ]
-    sems = [(6,), (8,), (8,), (), (), (), (), (), (2,), (), (), (2,), (2,), (), (2,), (2,), (2, 8)]
+    sems = [(6,), (16,), (8,), (8,), (), (), (), (), (), (4,), (), (2,), (2,), (2,), (), (2,), (2,), (2, 8)]
     return pl.pallas_call(
         kernel,
         name="monarch",
@@ -458,6 +531,7 @@
         in_specs=[any_space, vmem, any_space, any_space, any_space, any_space, vmem, vmem, any_space],
         out_specs=any_space,
         scratch_shapes=[pltpu.VMEM(*one) for one in scratch]
+        + [pltpu.SemaphoreType.REGULAR]
         + [dma(shape) if shape else dma for shape in sems],
         compiler_params=pltpu.CompilerParams(
             collective_id=0, has_side_effects=True, vmem_limit_bytes=60 << 20
@@ -466,11 +540,11 @@
         activations,
         conv_weight,
         chan_right.reshape(512, 64),
-        packed,
+        chan_left,
         row_factor,
         col_factor,
-        twiddle_one.T,
-        twiddle_two,
+        twiddle_one,
+        twiddle_two.T,
         spectrum,
     )
 

time: 273 us -> 246 us (0.901)
  the two profiles are of different devices: /device:TPU:1 before, /device:TPU:41 now
where the time goes in v3:
time: 246 us
  Pallas kernels  241 us (98%)
  local copies, waits for them, and re-layouts  4.47 us (2%)
    pallas_call x1, Pallas kernels, shards(): pl.pallas_call(kernel, name='monarch', out_shape=jax.ShapeDtypeStruct(act...  241 us

profile of v3, /device:TPU:41, one launch (start us, length us, event | category | flops | bytes accessed | tf_op | source)
XLA Modules:
  0.0 245.9 jit_solution(8748782911278387700)
XLA Ops:
  0.0 241.4 %monarch.1 = bf16[4096,512]{1,0:T(8,128)(2,1)} custom-call(bf16[4096,512]{1,0:T(8,128)(2,1)} %x_hbm.1, f32[3,512]{1,0:T(4,128)} %taps.1, bf16[512,64]{1,0:T(8,128)(2,1)} %bitcast.2, bf16[8,64,64]{2,1,0:T(8,128)(2,1)} %left_hbm.1, bf16[512,512]{1,0:T(8,128)(2,1)} %row_hbm.1, bf16[256,256]{1,0:T(8,128)(2,1)} %col_hbm.1, f32[8,512]{1,0:T(8,128)} %twiddle_one.1, ...), custom_call_target="tpu_custom_call" | custom-call | tf_op jit(solution)/shard_map/monarch/pallas_call | solution.py:527
  241.4 4.5 %copy.11 = bf16[4096,512]{1,0:T(8,128)(2,1)} copy(bf16[4096,512]{1,0:T(8,128)(2,1)} %monarch.1) | data formatting | bytes 8388608

commit v4 on v3

--- a/solution.py
+++ b/solution.py
@@ -22,29 +22,35 @@
     return jnp.where(condition, 1.0, 0.0).astype(BF16)
 
 
+def column(table, index):
+    return jnp.sum(jnp.where(iota(table.shape, 1) == index, table, 0.0), 1, keepdims=True)
+
+
 def wait_bytes(ref, sem):
     pltpu.make_async_copy(ref, ref, sem).wait()
 
 
 def kernel(
     x_hbm,
-    taps,
+    taps_hbm,
     right_hbm,
     left_hbm,
     row_hbm,
     col_hbm,
-    twiddle_one,
-    twiddle_two,
+    one_hbm,
+    two_hbm,
     spectrum_hbm,
     out_hbm,
     xw,
+    taps,
+    twiddle_one,
+    twiddle_two,
     right,
     left_raw,
     left_own,
     left_all,
-    row_n,
+    row_t,
     row_f,
-    row_t,
     col_f,
     col_t,
     swap,
@@ -53,8 +59,7 @@
     left_w,
     twiddle_n,
     twiddle_a,
-    twiddle_b,
-    gated,
+    twiddle_c,
     send_a,
     recv_a,
     mixed,
@@ -73,6 +78,8 @@
     halo_recv,
     left_send,
     left_recv,
+    pair_send,
+    pair_recv,
     a_send,
     a_recv,
     a_own,
@@ -102,14 +109,23 @@
     small = [
         pltpu.make_async_copy(src, dst, load_sem.at[i])
         for i, (src, dst) in enumerate(
-            ((right_hbm, right), (row_hbm, row_n), (col_hbm, col_f), (left_hbm, left_raw))
+            (
+                (right_hbm, right),
+                (row_hbm, row_t),
+                (col_hbm, col_f),
+                (left_hbm, left_raw),
+                (taps_hbm, taps),
+                (one_hbm, twiddle_one),
+                (two_hbm, twiddle_two),
+            )
         )
     ]
     for copy in small:
         copy.start()
 
-    blocks = [(2, 0), (2, 1), (1, 0), (1, 1), (1, 2), (1, 3), (0, 0), (0, 1)]
-    blocks += [(2, 2), (2, 3), (3, 0), (3, 1), (3, 2), (3, 3), (0, 2), (0, 3)]
+    upper = [(1, 0), (2, 0), (1, 1), (0, 0), (1, 2), (2, 1), (1, 3), (0, 1)]
+    lower = [(3, 0), (2, 2), (3, 1), (0, 2), (3, 2), (2, 3), (3, 3), (0, 3)]
+    blocks = upper + lower
 
     def block_rows(i):
         up, along = blocks[i]
@@ -138,7 +154,7 @@
         )
 
     def front_row(step):
-        return (y + 1 + step // 2) % 4 * 2 + step % 2
+        return (y + 1 + step // 2) % 4 * 2 + 1 - step % 2
 
     @pl.loop(0, 8)
     def _(step):
@@ -151,7 +167,7 @@
 
     kernel_copies = [
         pltpu.make_async_copy(
-            spectrum_hbm.at[:, :, pl.ds(256 * ch, 256)], send_c.at[ch], load_sem.at[4 + ch]
+            spectrum_hbm.at[:, :, pl.ds(256 * ch, 256)], send_c.at[ch], load_sem.at[7 + ch]
         )
         for ch in range(2)
     ]
@@ -176,13 +192,6 @@
     for i in range(16):
         twiddle_a[32 * i : 32 * i + 32] = twiddle_n[block_rows(i)]
 
-    pl.semaphore_wait(barrier, 38)
-
-    @pl.loop(0, 7)
-    def _(turn):
-        peer = (seq, mp_peer(turn))
-        pl.semaphore_signal(ready, inc=1, device_id=peer, device_id_type=MESH)
-
     halo = pltpu.make_async_remote_copy(
         src_ref=x_hbm.at[pl.ds(4080, 16)],
         dst_ref=xw.at[0, pl.ds(0, 16)],
@@ -191,7 +200,6 @@
         device_id=((seq + 1) % 32, mp),
         device_id_type=MESH,
     )
-    halo.start()
 
     def send_left():
         @pl.loop(0, 7)
@@ -200,8 +208,8 @@
             shift = jnp.where(turn < 4, jnp.where(z_lo == 1, 1, 3), 0)
             to_seq = (x * 4 + (z_hi + shift) % 4) * 2 + core
             pltpu.make_async_remote_copy(
-                src_ref=left_own,
-                dst_ref=left_all.at[mp],
+                src_ref=left_own.at[pl.ds(core * 2, 2)],
+                dst_ref=left_all.at[mp, pl.ds(core * 2, 2)],
                 send_sem=left_send,
                 recv_sem=left_recv,
                 device_id=(to_seq, peer),
@@ -215,7 +223,7 @@
             rows = pl.ds(pl.multiple_of((1 - to_z) * 256 + part * 64, 64), 64)
             pltpu.make_async_remote_copy(
                 src_ref=send_a.at[a, rows],
-                dst_ref=recv_a.at[mp, step % 2, pl.ds(part * 64, 64)],
+                dst_ref=recv_a.at[mp, a % 2, pl.ds(part * 64, 64)],
                 send_sem=a_send,
                 recv_sem=a_recv.at[part],
                 device_id=(seq, to_z * 4 + a // 2),
@@ -228,9 +236,7 @@
         def _():
             send(z_lo)
 
-    @pl.loop(0, 8)
-    def _(step):
-        a = front_row(step)
+    def front(a):
         x_copy(a).wait()
 
         @pl.when(a > 0)
@@ -253,18 +259,29 @@
             conv_out = (
                 taps[0:1] * here + taps[1:2] * window[15:143] + taps[2:3] * window[14:142]
             )
-            gated[pl.ds(start, 128)] = (here * conv_out / (1.0 + jnp.exp(-conv_out))).astype(BF16)
-
-        first = dot32(gated[...], right_w[...]).astype(BF16)
-        scale = jnp.sum(jnp.where(iota((512, 8), 1) == a, twiddle_a[...], 0.0), 1, keepdims=True)
-        send_a[a] = (dot32(row_f[...], first) * scale).astype(BF16)
-
+            mixed[pl.ds(start, 128), :512] = (here * conv_out / (1.0 + jnp.exp(-conv_out))).astype(BF16)
+
+        first = dot32(mixed[:, :512], right_w[...]).astype(BF16)
+        send_a[a] = (dot32(row_f[...], first) * column(twiddle_a[...], a)).astype(BF16)
+
+    front(front_row(0))
+
+    pl.semaphore_wait(barrier, 38)
+
+    @pl.loop(0, 7)
+    def _(turn):
+        peer = (seq, mp_peer(turn))
+        pl.semaphore_signal(ready, inc=1, device_id=peer, device_id_type=MESH)
+
+    halo.start()
+    send_rows(0, 0)
+    pl.semaphore_wait(ready, 7)
+    send_left()
+
+    @pl.loop(1, 8)
+    def _(step):
+        front(front_row(step))
         send_rows(step, 0)
-
-        @pl.when(step == 1)
-        def _():
-            pl.semaphore_wait(ready, 7)
-            send_left()
 
     own_rows = pltpu.make_async_copy(
         send_a.at[pl.ds(pl.multiple_of(2 * y, 2), 2), pl.ds(pl.multiple_of((1 - z_lo) * 256, 256), 256)],
@@ -278,15 +295,26 @@
         def _(step):
             send_rows(step, part)
 
-    row_t[...] = row_n[...].astype(F32).T.astype(BF16)
+    row_t[...] = row_t[...].astype(F32).T.astype(BF16)
     col_t[...] = col_f[...].astype(F32).T.astype(BF16)
     row, col = iota((256, 256), 0), iota((256, 256), 1)
     swap[...] = one_hot(row // 16 + row % 16 * 16 == col)
     row, col = iota((512, 512), 0), iota((512, 512), 1)
     natural[...] = one_hot(row // 16 % 8 * 64 + row // 128 * 16 + row % 16 == col)
 
-    left_all[mp] = left_own[...]
-    wait_bytes(left_all.at[pl.ds(0, 7)], left_recv)
+    halves = left_all.at[:, pl.ds(core * 2, 2)]
+    left_all[mp, pl.ds(core * 2, 2)] = left_own[pl.ds(core * 2, 2)]
+    wait_bytes(left_all.at[pl.ds(0, 7), pl.ds(0, 2)], left_recv)
+    to_pair = pltpu.make_async_remote_copy(
+        src_ref=halves,
+        dst_ref=halves,
+        send_sem=pair_send,
+        recv_sem=pair_recv,
+        device_id=(seq + 1 - 2 * core, mp),
+        device_id_type=MESH,
+    )
+    to_pair.start()
+    to_pair.wait_recv()
 
     @pl.loop(0, 8)
     def _(owner):
@@ -309,22 +337,22 @@
             turned = dot32(swap[...], send_c[ch, rows].reshape(256, 256)).astype(BF16)
             kernel_t[ch, :, rows] = turned.reshape(16, 16, 256)
 
-    scales = twiddle_two[...].T
-    for p in range(16):
-        twiddle_b[p] = jnp.broadcast_to(scales[:, p : p + 1], (256, 128))
+    twiddle_c[...] = twiddle_two[...].T
 
     own_rows.wait()
 
     first_a = pl.multiple_of(seq * 8 + y * 2, 2)
 
     def send_columns(ch, part, to_mp):
-        up = [2, 3 - 2 * z_lo, 3 - 2 * z_lo, 0][part]
-        along = [2 - 2 * z_lo, 0, 2, 2 - 2 * z_lo][part]
+        def steps(k, i):
+            high = jnp.where(i // 2 == 0, upper[2 * part][k], upper[2 * part + 1][k])
+            low = jnp.where(i // 2 == 0, lower[2 * part][k], lower[2 * part + 1][k])
+            return jnp.where(z_lo == 1, high, low)
 
         @pl.loop(0, 4)
         def _(i):
             to_core = (core + i) % 2
-            to_seq = ((x + along + i // 2) % 4 * 4 + (z_hi + up) % 4) * 2 + to_core
+            to_seq = ((x + steps(1, i)) % 4 * 4 + (z_hi + steps(0, i)) % 4) * 2 + to_core
             rows = pl.ds(pl.multiple_of(part * 64 + i // 2 * 32 + to_core * 16, 16), 16)
             src = send_b.at[ch, to_mp, :, rows]
             dst = recv_b.at[ch, pl.ds(first_a, 2)]
@@ -339,7 +367,7 @@
                     device_id_type=MESH,
                 ).start()
 
-            if part < 3:
+            if (0, 0) not in upper[2 * part : 2 * part + 2]:
                 remote()
             else:
                 own = jnp.logical_and(to_seq == seq, to_mp == mp)
@@ -365,16 +393,17 @@
                 ],
                 1,
             )
+            rows = pl.ds(pl.multiple_of(group * 128, 128), 128)
             for n in range(4):
                 cut = slice(256 * n, 256 * n + 256)
                 weights = left_w[group, :, :, cut].reshape(1024, 256)
-                mixed[group, :, cut] = dot32(block, weights).astype(BF16)
+                mixed[rows, cut] = dot32(block, weights).astype(BF16)
 
         @pl.loop(0, 8)
         def _(turn):
             to_mp = mp_peer(turn)
             lanes = pl.ds(pl.multiple_of(to_mp * 128, 128), 128)
-            block = jnp.concatenate([mixed[group, :, lanes] for group in range(4)], 1)
+            block = jnp.concatenate([mixed[128 * group : 128 * group + 128, lanes] for group in range(4)], 1)
             for ch in range(2):
                 cut = slice(256 * ch, 256 * ch + 256)
                 turned = dot32(block, natural[:, cut]).astype(BF16)
@@ -408,8 +437,7 @@
         def _(p):
             spectral = (dot32(col_f[...], columns[p]) * kernel_t[ch, p].astype(F32)).astype(BF16)
             back = dot32(col_t[...], spectral)
-            scale = twiddle_b[p]
-            columns[p] = (back * jnp.concatenate([scale, scale], 1)).astype(BF16)
+            columns[p] = (back * column(twiddle_c[...], p)).astype(BF16)
 
         @pl.loop(0, 16)
         def _(i):
@@ -447,6 +475,7 @@
             out_sem.at[ch, a],
         )
 
+
     for ch in range(2):
         wait_bytes(recv_c.at[ch, :, pl.ds(0, 496)], c_recv.at[ch])
         wait_bytes(recv_c.at[ch, :, pl.ds(0, 16)], c_own.at[ch])
@@ -465,7 +494,8 @@
             out_copy(ch, a).wait()
 
     halo.wait_send()
-    wait_bytes(left_all.at[pl.ds(0, 7)], left_send)
+    to_pair.wait_send()
+    wait_bytes(left_all.at[pl.ds(0, 7), pl.ds(0, 2)], left_send)
     for ch in range(2):
 
         @pl.when(z_lo == 1)
@@ -491,16 +521,17 @@
     twiddle_two,
     spectrum,
 ):
-    any_space = pl.BlockSpec(memory_space=pl.ANY)
-    vmem = pl.BlockSpec(memory_space=pltpu.VMEM)
+    hbm = pl.BlockSpec(memory_space=pltpu.HBM)
     dma = pltpu.SemaphoreType.DMA
     scratch = [
         ((8, 528, 512), BF16),
+        ((3, 512), F32),
+        ((8, 512), F32),
+        ((16, 256), F32),
         ((512, 64), BF16),
         ((8, 64, 64), BF16),
         ((4, 64, 128), BF16),
         ((8, 4, 64, 128), BF16),
-        ((512, 512), BF16),
         ((512, 512), BF16),
         ((512, 512), BF16),
         ((256, 256), BF16),
@@ -511,11 +542,10 @@
         ((4, 8, 128, 1024), BF16),
         ((512, 8), F32),
         ((512, 8), F32),
-        ((16, 256, 128), F32),
-        ((512, 512), BF16),
+        ((256, 16), F32),
         ((8, 512, 512), BF16),
         ((8, 2, 256, 512), BF16),
-        ((4, 128, 1024), BF16),
+        ((512, 1024), BF16),
         ((2, 8, 2, 256, 256), BF16),
         ((2, 256, 16, 256), BF16),
         ((16, 256, 256), BF16),
@@ -523,13 +553,13 @@
         ((2, 256, 16, 256), BF16),
         ((2, 8, 512, 256), BF16),
     ]
-    sems = [(6,), (16,), (8,), (8,), (), (), (), (), (), (4,), (), (2,), (2,), (2,), (), (2,), (2,), (2, 8)]
+    sems = [(9,), (16,), (8,), (8,), (), (), (), (), (), (), (), (4,), (), (2,), (2,), (2,), (), (2,), (2,), (2, 8)]
     return pl.pallas_call(
         kernel,
         name="monarch",
         out_shape=jax.ShapeDtypeStruct(activations.shape, activations.dtype),
-        in_specs=[any_space, vmem, any_space, any_space, any_space, any_space, vmem, vmem, any_space],
-        out_specs=any_space,
+        in_specs=[hbm] * 9,
+        out_specs=hbm,
         scratch_shapes=[pltpu.VMEM(*one) for one in scratch]
         + [pltpu.SemaphoreType.REGULAR]
         + [dma(shape) if shape else dma for shape in sems],

time: 246 us -> 239 us (0.972)
  the two profiles are of different devices: /device:TPU:41 before, /device:TPU:1 now
where the time goes in v4:
time: 239 us
  Pallas kernels  234 us (98%)
  local copies, waits for them, and re-layouts  4.47 us (2%)
    pallas_call x1, Pallas kernels, shards(): pl.pallas_call(kernel, name='monarch', out_shape=jax.ShapeDtypeStruct(act...  234 us

profile of v4, /device:TPU:1, one launch (start us, length us, event | category | flops | bytes accessed | tf_op | source)
XLA Modules:
  0.0 238.7 jit_solution(2700180264285269553)
XLA Ops:
  0.0 234.2 %monarch.1 = bf16[4096,512]{1,0:T(8,128)(2,1)} custom-call(bf16[4096,512]{1,0:T(8,128)(2,1)} %x_hbm.1, f32[3,512]{1,0:T(4,128)} %taps_hbm.1, bf16[512,64]{1,0:T(8,128)(2,1)} %bitcast.2, bf16[8,64,64]{2,1,0:T(8,128)(2,1)} %left_hbm.1, bf16[512,512]{1,0:T(8,128)(2,1)} %row_hbm.1, bf16[256,256]{1,0:T(8,128)(2,1)} %col_hbm.1, f32[8,512]{1,0:T(8,128)} %one_hbm.1, ...), custom_call_target="tpu_custom_call" | custom-call | tf_op jit(solution)/shard_map/monarch/pallas_call | solution.py:557
  234.2 4.5 %copy.11 = bf16[4096,512]{1,0:T(8,128)(2,1)} copy(bf16[4096,512]{1,0:T(8,128)(2,1)} %monarch.1) | data formatting | bytes 8388608

commit v5 on v4

--- a/solution.py
+++ b/solution.py
@@ -410,7 +410,7 @@
                 send_b[ch, to_mp, :, 64 * part : 64 * part + 64] = turned.reshape(2, 64, 256)
             send_columns(0, part, to_mp)
 
-        for late in {0: [0], 3: [1, 2, 3]}.get(part, []):
+        for late in {3: [0, 1, 2, 3]}.get(part, []):
 
             @pl.loop(0, 8)
             def _(turn):
@@ -441,7 +441,7 @@
 
         @pl.loop(0, 16)
         def _(i):
-            block = (seq // 2 + i) % 16
+            block = (seq // 2 + 1 + i) % 16
             rows = pl.ds(pl.multiple_of(block * 16, 16), 16)
             turned = dot32(swap[...], columns[:, rows].reshape(256, 256)).astype(BF16)
             send_c[ch, rows] = turned.reshape(16, 16, 256)

time: 239 us -> 245 us (1.025)
  Pallas kernels: 234 us -> 240 us
    pallas_call x1, Pallas kernels: 234 us -> 240 us  [shards(): pl.pallas_call(kernel, name='monarch', out_shape=jax.ShapeDtypeStruct(act...]
where the time goes in v5:
time: 245 us
  Pallas kernels  240 us (98%)
  local copies, waits for them, and re-layouts  4.47 us (2%)
    pallas_call x1, Pallas kernels, shards(): pl.pallas_call(kernel, name='monarch', out_shape=jax.ShapeDtypeStruct(act...  240 us

profile of v5, /device:TPU:1, one launch (start us, length us, event | category | flops | bytes accessed | tf_op | source)
XLA Modules:
  0.0 244.7 jit_solution(16892032123625382532)
XLA Ops:
  0.0 240.2 %monarch.1 = bf16[4096,512]{1,0:T(8,128)(2,1)} custom-call(bf16[4096,512]{1,0:T(8,128)(2,1)} %x_hbm.1, f32[3,512]{1,0:T(4,128)} %taps_hbm.1, bf16[512,64]{1,0:T(8,128)(2,1)} %bitcast.2, bf16[8,64,64]{2,1,0:T(8,128)(2,1)} %left_hbm.1, bf16[512,512]{1,0:T(8,128)(2,1)} %row_hbm.1, bf16[256,256]{1,0:T(8,128)(2,1)} %col_hbm.1, f32[8,512]{1,0:T(8,128)} %one_hbm.1, ...), custom_call_target="tpu_custom_call" | custom-call | tf_op jit(solution)/shard_map/monarch/pallas_call | solution.py:557
  240.2 4.5 %copy.11 = bf16[4096,512]{1,0:T(8,128)(2,1)} copy(bf16[4096,512]{1,0:T(8,128)(2,1)} %monarch.1) | data formatting | bytes 8388608
